TPU v7x, 1024 devices: a whole 4x8x16 slice. The times are simulated.
1024 devices in a mesh: grp: 16 (over y, core), gx: 64 (over x, z).
Axes of the slice: x: 4, y: 8, z: 16, core: 2. Of those that a mesh axis runs over, the one named last changes fastest.
Arguments:
- voltages: bfloat16 [16, 512, 2, 1, 2, 16384], P('grp', 'gx'), may hold values from -6 to 6
- tile_of: int32 [16, 32768], P(None, 'gx'), may hold values from -1 to 15, as said below
- cell_of: int32 [16, 32768], P(None, 'gx'), may hold values from 0 to 127
Outputs:
- image: float32 [16, 2, 4096, 4096], P('grp', None, 'gx')
Inputs may be any that keep to these rules, and one draw needn't show every extreme that they name: `tile_of`: among the 512 blocks of one coarse channel and one gx index, no tile is named more than 8 times, and one tile exactly 8 times; -1 marks blocks that no tile takes.
All inputs are finite; a program needn't handle non-finite values.
Results may differ from a plain program's by a relative error of at most 0.006.
Values may be sent and summed in bfloat16 or wider, within the bound.
A program may use at most 64 MiB of HBM per device.

v0:
```python
import functools
import math

import jax
import jax.numpy as jnp
import numpy as np
from jax import lax
from jax.experimental import pallas as pl
from jax.experimental.pallas import tpu as pltpu
from jax.sharding import PartitionSpec as P

F32 = jnp.float32
BF16 = jnp.bfloat16
MESH = pl.DeviceIdType.MESH
VMEM_LIMIT = 56 * 1024 * 1024


def split(table):
    high = table.astype(np.float32).astype(jnp.bfloat16)
    low = (table - high.astype(np.float64)).astype(np.float32).astype(jnp.bfloat16)
    return high, low


def turn(left, right, size, sign):
    angle = sign * 2.0 * math.pi / size * (np.outer(left, right) % size)
    return np.cos(angle), np.sin(angle)


@functools.cache
def tables():
    made = {}
    i128 = np.arange(128)
    c, s = turn(i128, i128, 128, -1)
    m1 = np.zeros((2, 128, 128, 2))
    m1[0, :, :, 0], m1[0, :, :, 1] = c, -s
    m1[1, :, :, 0], m1[1, :, :, 1] = s, c
    made["m1"] = np.concatenate(split(m1.reshape(256, 256)))
    made["tw1"] = np.stack(turn(i128, i128, 16384, -1)).astype(np.float32)
    c, s = turn(i128, i128, 128, -1)
    c, s = (t.reshape(64, 2, 128).transpose(1, 0, 2).reshape(128, 128) / 128.0 for t in (c, s))
    made["v1"] = np.concatenate(split(np.block([[c, -s], [s, c]])))
    c, s = turn(np.arange(32), np.arange(32), 32, 1)
    w = np.zeros((2, 4, 32, 2, 4, 32))
    for rb in range(4):
        w[0, rb, :, 0, rb], w[0, rb, :, 1, rb] = c, -s
        w[1, rb, :, 0, rb], w[1, rb, :, 1, rb] = s, c
    made["w"] = np.concatenate(split(w.reshape(256, 256)))
    tw = np.stack(turn(np.arange(32), i128, 4096, 1))
    made["tw2"] = np.tile(tw, (1, 4, 1)).astype(np.float32)
    c, s = turn(i128, i128, 128, 1)
    c, s = (t.reshape(64, 2, 128).transpose(1, 0, 2).reshape(128, 128) / 64.0 for t in (c, s))
    made["v2"] = np.concatenate(split(np.block([[c, -s], [s, c]])))
    n1 = (2 * np.arange(64)[None, :] + np.arange(2)[:, None]).reshape(128)
    c, s = turn(n1, i128, 128, 1)
    made["m4"] = np.concatenate(split(np.block([[c, s], [-s, c]])), axis=1)
    n0 = np.arange(32)
    tw = np.stack(turn(n0, i128, 4096, 1)).reshape(2, 2, 16, 1, 128)
    made["tw4"] = np.broadcast_to(tw, (2, 2, 16, 8, 128)).reshape(2, 2, 128, 128).astype(np.float32)
    c, s = turn(n0, n0, 32, 1)
    v4 = np.block([[c, -s], [s, c]]) / 64.0
    made["v4"] = np.concatenate(split(np.kron(v4, np.eye(8))))
    return made


def nt(left, right):
    return lax.dot_general(left, right, (((1,), (1,)), ((), ())), preferred_element_type=F32)


def tn(left, right):
    return lax.dot_general(left, right, (((0,), (0,)), ((), ())), preferred_element_type=F32)


def nn(left, right):
    return jnp.dot(left, right, preferred_element_type=F32)


def route_kernel(tile_ref, cell_ref, w_ref, idx_ref, place_ref):
    me = lax.axis_index("grp")
    tiles = tile_ref[...]
    mine = tile_ref[pl.ds(me, 1), :]
    marks = jnp.concatenate(
        [mine == lax.broadcasted_iota(jnp.int32, (16, 512), 0), tiles == me], axis=0
    ).astype(F32)
    before = lax.broadcasted_iota(jnp.int32, (512, 512), 0) < lax.broadcasted_iota(
        jnp.int32, (512, 512), 1
    )
    rank = nn(marks.astype(BF16), before.astype(F32).astype(BF16))
    rank = jnp.where(marks > 0.5, rank, -1.0).astype(jnp.int32)
    position = lax.broadcasted_iota(jnp.int32, (16, 512), 1)
    columns = [
        jnp.sum(jnp.where(rank[:16] == k, position, 0), axis=1, keepdims=True) for k in range(8)
    ]
    idx_ref[...] = jnp.concatenate(columns, axis=1)
    slot = lax.broadcasted_iota(jnp.int32, (8, 512), 0)
    lane = lax.broadcasted_iota(jnp.int32, (8, 256), 1)
    hits = []
    for g in range(16):
        chosen = rank[16 + g : 17 + g] == slot
        cell = jnp.sum(jnp.where(chosen, cell_ref[g : g + 1, :] + 1, 0), axis=1, keepdims=True) - 1
        for part in range(2):
            at = jnp.where(cell < 0, -1, cell + 128 * part)
            hits.append((lane == at).astype(F32))
    onehot = jnp.concatenate(hits, axis=0).astype(BF16)
    place_ref[...] = nt(w_ref[...], onehot).astype(BF16)


def partner(me, step):
    dx = lax.rem(step, 4)
    d = step // 4
    up = (d + 1) // 2
    dz = jnp.where(lax.rem(d, 2) == 1, up, 16 - up)
    x, z = me // 16, lax.rem(me, 16)
    to = lax.rem(x + dx, 4) * 16 + lax.rem(z + dz, 16)
    source = lax.rem(x + 4 - dx, 4) * 16 + lax.rem(z + 16 - lax.rem(dz, 16), 16)
    return to, source


def greet_gx(me):
    barrier = pltpu.get_barrier_semaphore()

    def hello(step, carry):
        to, _ = partner(me, step)
        pl.semaphore_signal(barrier, inc=1, device_id={"gx": to}, device_id_type=MESH)
        return carry

    lax.fori_loop(1, 64, hello, 0)


def gx_copy(send_ref, recv_ref, send_sem, recv_sem, to, slot):
    return pltpu.make_async_remote_copy(
        src_ref=send_ref.at[to],
        dst_ref=recv_ref.at[slot],
        send_sem=send_sem.at[to],
        recv_sem=recv_sem.at[slot],
        device_id={"gx": to},
        device_id_type=MESH,
    )


def spectra_phase(x_ref, m1_ref, tw_ref, v_ref, z_ref):
    def pair(h, carry):
        x = jnp.concatenate([x_ref[2 * h], x_ref[2 * h + 1]], axis=1)
        y = nn(m1_ref[...], x)
        y = y[:256] + y[256:]
        for o in range(2):
            q = 2 * h + o
            re, im = y[:128, o * 128 : o * 128 + 128], y[128:, o * 128 : o * 128 + 128]
            cos, sin = tw_ref[0], tw_ref[1]
            both = jnp.concatenate([re * cos - im * sin, re * sin + im * cos], axis=1)
            high = both.astype(BF16)
            low = (both - high.astype(F32)).astype(BF16)
            out = nt(v_ref[...], high)
            out = out[:256] + out[256:] + nt(v_ref[:256], low)
            for s in range(4):
                z_ref[pl.ds(s * 16 + q, 64, stride=64), :] = out[s * 64 : s * 64 + 64]
        return carry

    lax.fori_loop(0, 8, pair, 0)


def operand(recv_ref, at):
    return jnp.concatenate(
        [recv_ref[pl.ds(at * 16, 16), s * 16 : s * 16 + 16, :].reshape(256, 128) for s in range(4)],
        axis=1,
    )


def gram_phase(recv_ref, vis_ref):
    def column(p, carry):
        right = operand(recv_ref, p)
        crossed = jnp.concatenate([-right[:, 256:], right[:, :256]], axis=1)

        def row(r, inner):
            left = operand(recv_ref, r)
            for part, other in enumerate((right, crossed)):
                out = nt(left, other)
                for half in range(2):
                    vis_ref[pl.ds(r * 16, 16), 2 * p + half, part * 16 : part * 16 + 16, :] = out[
                        :, half * 128 : half * 128 + 128
                    ].reshape(16, 16, 128)
            return inner

        lax.fori_loop(0, 4, row, 0)
        return carry

    lax.fori_loop(0, 4, column, 0)


def gather_phase(idx_ref, vis_ref, o_ref, out_ref):
    def tile(t, carry):
        for k in range(8):
            b = idx_ref[t, k]
            block = vis_ref[b // 8, b % 8]
            for part in range(2):
                o_ref[pl.ds(t * 256 + part * 8 + k, 16, stride=16), :] = block[
                    part * 16 : part * 16 + 16
                ]
        out_ref[t] = (o_ref[pl.ds(t * 256, 256), :] * 0.0625).astype(BF16)
        return carry

    lax.fori_loop(0, 16, tile, 0)


def correlate_kernel(
    x_ref, m1_ref, tw_ref, v_ref, idx_ref, out_ref, z_ref, vis_ref, send_ref, recv_ref, send_sem, recv_sem
):
    me = lax.axis_index("gx")
    greet_gx(me)
    spectra_phase(x_ref, m1_ref, tw_ref, v_ref, z_ref)
    pl.semaphore_wait(pltpu.get_barrier_semaphore(), 63)

    def push(step, carry):
        to, _ = partner(me, step)
        send_ref[to] = z_ref[pl.ds(pl.multiple_of(to * 64, 64), 64), :].astype(BF16)
        gx_copy(send_ref, recv_ref, send_sem, recv_sem, to, me).start()
        return carry

    lax.fori_loop(1, 64, push, 0)
    recv_ref[me] = z_ref[pl.ds(pl.multiple_of(me * 64, 64), 64), :].astype(BF16)

    def take(step, carry):
        to, source = partner(me, step)
        gx_copy(send_ref, recv_ref, send_sem, recv_sem, to, source).wait()
        return carry

    lax.fori_loop(1, 64, take, 0)
    gram_phase(recv_ref, vis_ref)
    gather_phase(idx_ref, vis_ref, z_ref, out_ref)


def rows_phase(got_ref, place_ref, tw_ref, v_ref, y_ref, z_ref):
    def line(i, carry):
        block = got_ref[:, pl.ds(pl.multiple_of(i * 16, 16), 16), :].reshape(256, 128)
        y = nn(place_ref[...], block)
        y = y[:256] + y[256:]
        re, im = y[:128], y[128:]
        cos, sin = tw_ref[0], tw_ref[1]
        at = pl.ds(pl.multiple_of(i * 8, 8), 8)
        y_ref[:, at, 0:128] = (re * cos - im * sin).reshape(16, 8, 128)
        y_ref[:, at, 128:256] = (re * sin + im * cos).reshape(16, 8, 128)
        return carry

    lax.fori_loop(0, 16, line, 0, unroll=2)

    def second(m, carry):
        out = nt(v_ref[...], y_ref[m].astype(BF16))
        out = out[:256] + out[256:]
        for s in range(4):
            z_ref[pl.ds(m * 4 + s, 64, stride=64), :] = out[s * 64 : s * 64 + 64]
        return carry

    lax.fori_loop(0, 16, second, 0, unroll=2)


def rows_kernel(
    blocks_ref, place_ref, tw_ref, v_ref, out_ref,
    got_ref, y_ref, z_ref, x_ref, send_ref, recv_ref, bsend_sem, brecv_sem, send_sem, recv_sem,
):
    me = lax.axis_index("gx")
    grp = lax.axis_index("grp")
    barrier = pltpu.get_barrier_semaphore()

    def hello(step, carry):
        to = lax.rem(grp + step, 16)
        pl.semaphore_signal(barrier, inc=1, device_id={"grp": to}, device_id_type=MESH)
        return carry

    lax.fori_loop(1, 16, hello, 0)
    greet_gx(me)
    pl.semaphore_wait(barrier, 78)

    def block_copy(to, slot):
        return pltpu.make_async_remote_copy(
            src_ref=blocks_ref.at[to],
            dst_ref=got_ref.at[slot],
            send_sem=bsend_sem.at[to],
            recv_sem=brecv_sem.at[slot],
            device_id={"grp": to},
            device_id_type=MESH,
        )

    def push_blocks(step, carry):
        block_copy(lax.rem(grp + step, 16), grp).start()
        return carry

    lax.fori_loop(1, 16, push_blocks, 0)
    got_ref[grp] = blocks_ref[grp]

    def take_blocks(step, carry):
        block_copy(lax.rem(grp + step, 16), lax.rem(grp + 16 - step, 16)).wait()
        return carry

    lax.fori_loop(1, 16, take_blocks, 0)
    rows_phase(got_ref, place_ref, tw_ref, v_ref, y_ref, z_ref)

    def push(step, carry):
        to, _ = partner(me, step)
        send_ref[to] = z_ref[pl.ds(pl.multiple_of(to * 64, 64), 64), :].astype(BF16)
        gx_copy(send_ref, recv_ref, send_sem, recv_sem, to, me).start()
        return carry

    lax.fori_loop(1, 64, push, 0)
    own = z_ref[pl.ds(pl.multiple_of(me * 64, 64), 64), :].astype(BF16)
    x_ref[pl.ds(me, 64, stride=64), :] = own.astype(F32)

    def take(step, carry):
        to, source = partner(me, step)
        gx_copy(send_ref, recv_ref, send_sem, recv_sem, to, source).wait()
        x_ref[pl.ds(source, 64, stride=64), :] = recv_ref[source].astype(F32)
        return carry

    lax.fori_loop(1, 64, take, 0)
    out_ref[...] = x_ref[...].astype(BF16)


def columns_kernel(x_ref, m4_ref, tw_ref, v_ref, image_ref):
    def eight(h, carry):
        k2, k1 = h // 4, h % 4
        turned = []
        for n in range(2):
            x = jnp.concatenate(
                [
                    x_ref[(2 * bit + n) * 16 + k1 * 4 + part * 2 + k2]
                    for part in range(2)
                    for bit in range(2)
                ],
                axis=0,
            )
            t = tn(x, m4_ref[...])
            t = t[:, :256] + t[:, 256:]
            re, im = t[:, :128], t[:, 128:]
            cos, sin = tw_ref[0, n], tw_ref[1, n]
            turned.append((re * cos - im * sin, re * sin + im * cos))
        t = jnp.concatenate([turned[0][0], turned[1][0], turned[0][1], turned[1][1]], axis=0)
        out = nn(v_ref[...], t.astype(BF16))
        out = out[:512] + out[512:]
        for part in range(2):
            for k in range(32):
                image_ref[part, pl.ds(pl.multiple_of(h * 8, 8), 8), k * 128 : k * 128 + 128] = out[
                    (part * 32 + k) * 8 : (part * 32 + k) * 8 + 8
                ]
        return carry

    lax.fori_loop(0, 8, eight, 0)


def params(**more):
    return pltpu.CompilerParams(vmem_limit_bytes=VMEM_LIMIT, **more)


def on_device(voltages, tile_of, cell_of):
    tab = {name: jnp.asarray(value) for name, value in tables().items()}
    vmem = pl.BlockSpec(memory_space=pltpu.VMEM)
    smem = pl.BlockSpec(memory_space=pltpu.SMEM)
    idx, place = pl.pallas_call(
        route_kernel,
        out_shape=(
            jax.ShapeDtypeStruct((16, 8), jnp.int32),
            jax.ShapeDtypeStruct((512, 256), BF16),
        ),
        compiler_params=params(),
        name="route",
    )(tile_of, cell_of, tab["w"])
    volts = voltages.reshape(16, 2, 128, 128).transpose(0, 2, 1, 3).reshape(16, 256, 128)
    blocks = pl.pallas_call(
        correlate_kernel,
        out_shape=jax.ShapeDtypeStruct((16, 256, 128), BF16),
        in_specs=[vmem] * 4 + [smem],
        out_specs=vmem,
        scratch_shapes=[
            pltpu.VMEM((4096, 128), F32),
            pltpu.VMEM((64, 8, 32, 128), F32),
            pltpu.VMEM((64, 64, 128), BF16),
            pltpu.VMEM((64, 64, 128), BF16),
            pltpu.SemaphoreType.DMA((64,)),
            pltpu.SemaphoreType.DMA((64,)),
        ],
        compiler_params=params(collective_id=0, has_side_effects=True),
        name="correlate",
    )(volts, tab["m1"], tab["tw1"], tab["v1"], idx)
    columns = pl.pallas_call(
        rows_kernel,
        out_shape=jax.ShapeDtypeStruct((4096, 128), BF16),
        in_specs=[vmem] * 4,
        out_specs=vmem,
        scratch_shapes=[
            pltpu.VMEM((16, 256, 128), BF16),
            pltpu.VMEM((16, 128, 256), F32),
            pltpu.VMEM((4096, 128), F32),
            pltpu.VMEM((4096, 128), F32),
            pltpu.VMEM((64, 64, 128), BF16),
            pltpu.VMEM((64, 64, 128), BF16),
            pltpu.SemaphoreType.DMA((16,)),
            pltpu.SemaphoreType.DMA((16,)),
            pltpu.SemaphoreType.DMA((64,)),
            pltpu.SemaphoreType.DMA((64,)),
        ],
        compiler_params=params(collective_id=1, has_side_effects=True),
        name="rows",
    )(blocks, place, tab["tw2"], tab["v2"])
    image = pl.pallas_call(
        columns_kernel,
        out_shape=jax.ShapeDtypeStruct((2, 64, 4096), F32),
        in_specs=[vmem] * 4,
        out_specs=vmem,
        compiler_params=params(),
        name="columns",
    )(columns.reshape(64, 64, 128), tab["m4"], tab["tw4"], tab["v4"])
    return image.reshape(1, 2, 64, 4096)


def solution(mesh):
    in_specs = (P("grp", "gx", None, None, None, None), P(None, "gx"), P(None, "gx"))
    out_specs = P("grp", None, "gx", None)
    return jax.shard_map(
        on_device, mesh=mesh, in_specs=in_specs, out_specs=out_specs, check_vma=False
    )
```

profile of v0, /device:TPU:1, one launch (start us, length us, event | category | flops | bytes accessed | tf_op | source)
XLA Modules:
  0.0 194.0 jit_solution(15071683218865442962)
XLA Ops:
  0.0 2.3 %route.1 = (s32[16,8]{1,0:T(8,128)}, bf16[512,256]{1,0:T(8,128)(2,1)}) custom-call(s32[16,512]{1,0:T(8,128)} %tile_ref.1, s32[16,512]{1,0:T(8,128)} %cell_ref.1, bf16[512,256]{1,0:T(8,128)(2,1)} %constant.21.clone.w_ref), custom_call_target="tpu_custom_call" | custom-call | tf_op jit(solution)/shard_map/route/pallas_call | solution.py:355
  2.3 76.0 %correlate.1.blocks_ref = bf16[16,256,128]{2,1,0:T(8,128)(2,1)} custom-call(bf16[16,256,128]{2,1,0:T(8,128)(2,1)} %bitcast.8, bf16[512,256]{1,0:T(8,128)(2,1)} %constant.18.clone.m1_ref, f32[2,128,128]{2,1,0:T(8,128)} %constant.19.clone.tw_ref, bf16[512,256]{1,0:T(8,128)(2,1)} %constant.20.clone.v_ref, s32[16,8]{1,0:T(8,128)} %get-tuple-element.7.idx_ref), custom_call_target="tpu_custom_call" | custom-call | tf_op jit(solution)/shard_map/correlate/pallas_call | solution.py:365
  78.2 107.3 %rows.1 = bf16[4096,128]{1,0:T(8,128)(2,1)} custom-call(bf16[16,256,128]{2,1,0:T(8,128)(2,1)} %correlate.1.blocks_ref, bf16[512,256]{1,0:T(8,128)(2,1)} %get-tuple-element.8.place_ref, f32[2,128,128]{2,1,0:T(8,128)} %constant.22.clone.tw_ref, bf16[512,256]{1,0:T(8,128)(2,1)} %constant.23.clone.v_ref), custom_call_target="tpu_custom_call" | custom-call | tf_op jit(solution)/shard_map/rows/pallas_call | solution.py:381
  185.5 8.5 %columns.1 = f32[2,64,4096]{2,1,0:T(8,128)} custom-call(bf16[64,64,128]{2,1,0:T(8,128)(2,1)} %bitcast.7, bf16[256,512]{1,0:T(8,128)(2,1)} %constant.24.clone.m4_ref, f32[2,2,128,128]{3,2,1,0:T(8,128)} %constant.25.clone.tw_ref, bf16[1024,512]{1,0:T(8,128)(2,1)} %constant.26.clone.v_ref), custom_call_target="tpu_custom_call" | custom-call | tf_op jit(solution)/shard_map/columns/pallas_call | solution.py:401
where the time goes:
time: 194 us
  Pallas kernels  194 us (100%)
    pallas_call x1, Pallas kernels, on_device(): pl.pallas_call(rows_kernel, out_shape=jax.ShapeDtypeStruct((4096, 128), B...  107 us
    pallas_call x1, Pallas kernels, on_device(): pl.pallas_call(correlate_kernel, out_shape=jax.ShapeDtypeStruct((16, 256,...  76 us
    pallas_call x1, Pallas kernels, on_device(): pl.pallas_call(columns_kernel, out_shape=jax.ShapeDtypeStruct((2, 64, 409...  8.48 us

commit v1 on v0

v1 whole, which is shorter than its diff:
```python
import functools
import math

import jax
import jax.numpy as jnp
import numpy as np
from jax import lax
from jax.experimental import pallas as pl
from jax.experimental.pallas import tpu as pltpu
from jax.sharding import PartitionSpec as P

F32 = jnp.float32
BF16 = jnp.bfloat16
MESH = pl.DeviceIdType.MESH


def split(table):
    high = table.astype(np.float32).astype(jnp.bfloat16)
    low = (table - high.astype(np.float64)).astype(np.float32).astype(jnp.bfloat16)
    return high, low


def turn(left, right, size, sign):
    angle = sign * 2.0 * math.pi / size * (np.outer(left, right) % size)
    return np.cos(angle), np.sin(angle)


@functools.cache
def tables():
    made = {}
    i128 = np.arange(128)
    c, s = turn(i128, i128, 128, -1)
    m1 = np.zeros((2, 128, 128, 2))
    m1[0, :, :, 0], m1[0, :, :, 1] = c, -s
    m1[1, :, :, 0], m1[1, :, :, 1] = s, c
    made["m1"] = np.concatenate(split(m1.reshape(256, 256)))
    made["tw1"] = np.stack(turn(i128, i128, 16384, -1)).astype(np.float32)
    c, s = turn(i128, i128, 128, -1)
    c, s = (t.reshape(64, 2, 128).transpose(1, 0, 2).reshape(128, 128) / 128.0 for t in (c, s))
    made["v1"] = np.concatenate(split(np.block([[c, -s], [s, c]])))
    c, s = turn(np.arange(32), np.arange(32), 32, 1)
    w = np.zeros((2, 4, 32, 2, 4, 32))
    for rb in range(4):
        w[0, rb, :, 0, rb], w[0, rb, :, 1, rb] = c, -s
        w[1, rb, :, 0, rb], w[1, rb, :, 1, rb] = s, c
    made["w"] = np.concatenate(split(w.reshape(256, 256)))
    tw = np.stack(turn(np.arange(32), i128, 4096, 1))
    made["tw2"] = np.tile(tw, (1, 4, 1)).astype(np.float32)
    c, s = turn(i128, i128, 128, 1)
    c, s = (t.reshape(64, 2, 128).transpose(1, 0, 2).reshape(128, 128) / 64.0 for t in (c, s))
    made["v2"] = np.concatenate(split(np.block([[c, -s], [s, c]])))
    n1 = (2 * np.arange(64)[None, :] + np.arange(2)[:, None]).reshape(128)
    c, s = turn(n1, i128, 128, 1)
    made["m4"] = np.concatenate(split(np.block([[c, s], [-s, c]])), axis=1)
    n0 = np.arange(32)
    tw = np.stack(turn(n0, i128, 4096, 1)).reshape(2, 4, 8, 1, 128)
    made["tw4"] = np.broadcast_to(tw, (2, 4, 8, 16, 128)).reshape(2, 4, 128, 128).astype(np.float32)
    c, s = turn(n0, n0, 32, 1)
    v4 = np.block([[c, -s], [s, c]]) / 64.0
    made["v4"] = np.concatenate(split(np.kron(v4, np.eye(8))))
    return made


def nt(left, right):
    return lax.dot_general(left, right, (((1,), (1,)), ((), ())), preferred_element_type=F32)


def tn(left, right):
    return lax.dot_general(left, right, (((0,), (0,)), ((), ())), preferred_element_type=F32)


def nn(left, right):
    return jnp.dot(left, right, preferred_element_type=F32)


def route_phase(me, tile_ref, cell_ref, w_ref, idx_ref, place_ref):
    tiles = tile_ref[...]
    mine = tile_ref[pl.ds(me, 1), :]
    marks = jnp.concatenate(
        [mine == lax.broadcasted_iota(jnp.int32, (16, 512), 0), tiles == me], axis=0
    ).astype(F32)
    before = lax.broadcasted_iota(jnp.int32, (512, 512), 0) < lax.broadcasted_iota(
        jnp.int32, (512, 512), 1
    )
    rank = nn(marks.astype(BF16), before.astype(F32).astype(BF16))
    rank = jnp.where(marks > 0.5, rank, -1.0).astype(jnp.int32)
    position = lax.broadcasted_iota(jnp.int32, (16, 512), 1)
    columns = [
        jnp.sum(jnp.where(rank[:16] == k, position, 0), axis=1, keepdims=True) for k in range(8)
    ]
    idx_ref[...] = jnp.concatenate(columns + [columns[0]] * 120, axis=1)
    slot = lax.broadcasted_iota(jnp.int32, (8, 512), 0)
    lane = lax.broadcasted_iota(jnp.int32, (8, 256), 1)
    hits = []
    for g in range(16):
        chosen = rank[16 + g : 17 + g] == slot
        cell = jnp.sum(jnp.where(chosen, cell_ref[g : g + 1, :] + 1, 0), axis=1, keepdims=True) - 1
        for part in range(2):
            at = jnp.where(cell < 0, -1, cell + 128 * part)
            hits.append((lane == at).astype(F32))
    onehot = jnp.concatenate(hits, axis=0).astype(BF16)
    place_ref[...] = nt(w_ref[...], onehot).astype(BF16)


def partner(me, dx, d):
    up = (d + 1) // 2
    dz = jnp.where(lax.rem(d, 2) == 1, up, lax.rem(16 - up, 16))
    x, z = me // 16, lax.rem(me, 16)
    to = lax.rem(x + dx, 4) * 16 + lax.rem(z + dz, 16)
    source = lax.rem(x + 4 - dx, 4) * 16 + lax.rem(z + 16 - dz, 16)
    return to, source


def by_row(me, step):
    return partner(me, step // 16, lax.rem(step, 16))


def by_distance(me, step):
    return partner(me, lax.rem(step, 4), step // 4)


def gx_copy(send_ref, recv_ref, send_sem, recv_sem, to, slot):
    return pltpu.make_async_remote_copy(
        src_ref=send_ref.at[to],
        dst_ref=recv_ref.at[slot],
        send_sem=send_sem.at[to],
        recv_sem=recv_sem.at[slot],
        device_id={"gx": to},
        device_id_type=MESH,
    )


def grp_copy(send_ref, recv_ref, send_sem, recv_sem, to, slot):
    return pltpu.make_async_remote_copy(
        src_ref=send_ref.at[to],
        dst_ref=recv_ref.at[slot],
        send_sem=send_sem.at[to],
        recv_sem=recv_sem.at[slot],
        device_id={"grp": to},
        device_id_type=MESH,
    )


def greet(me, grp):
    barrier = pltpu.get_barrier_semaphore()

    def along_gx(step, carry):
        to, _ = by_row(me, step)
        pl.semaphore_signal(barrier, inc=1, device_id={"gx": to}, device_id_type=MESH)
        return carry

    lax.fori_loop(1, 64, along_gx, 0)

    def along_grp(step, carry):
        to = lax.rem(grp + step, 16)
        pl.semaphore_signal(barrier, inc=1, device_id={"grp": to}, device_id_type=MESH)
        return carry

    lax.fori_loop(1, 16, along_grp, 0)


def spectra_phase(x_ref, m1_ref, tw_ref, v_ref, z_ref):
    def pair(h, carry):
        x = jnp.concatenate([x_ref[2 * h], x_ref[2 * h + 1]], axis=1)
        y = nn(m1_ref[...], x)
        y = y[:256] + y[256:]
        cos, sin = tw_ref[0], tw_ref[1]
        both = []
        for o in range(2):
            re, im = y[:128, o * 128 : o * 128 + 128], y[128:, o * 128 : o * 128 + 128]
            both.append(jnp.concatenate([re * cos - im * sin, re * sin + im * cos], axis=1))
        both = jnp.concatenate(both, axis=0)
        high = both.astype(BF16)
        low = (both - high.astype(F32)).astype(BF16)
        out = nt(v_ref[...], high)
        out = out[:256] + out[256:] + nt(v_ref[:256], low)
        for o in range(2):
            for s in range(4):
                z_ref[pl.ds(s * 16 + 2 * h + o, 64, stride=64), :] = out[
                    s * 64 : s * 64 + 64, o * 128 : o * 128 + 128
                ]
        return carry

    lax.fori_loop(0, 8, pair, 0)


def operand(recv_ref, at):
    return jnp.concatenate(
        [recv_ref[pl.ds(at * 16, 16), s * 16 : s * 16 + 16, :].reshape(256, 128) for s in range(4)],
        axis=1,
    )


def gram_block(recv_ref, vis_ref, r, p):
    left, right = operand(recv_ref, r), operand(recv_ref, p)
    crossed = jnp.concatenate([-right[:, 256:], right[:, :256]], axis=1)
    for part, other in enumerate((right, crossed)):
        out = nt(left, other)
        for half in range(2):
            vis_ref[pl.ds(r * 16, 16), 2 * p + half, part * 16 : part * 16 + 16, :] = out[
                :, half * 128 : half * 128 + 128
            ].reshape(16, 16, 128)


def gather_phase(h, idx_ref, vis_ref, z_ref, out_ref):
    def tile(t, carry):
        for k in range(8):
            b = idx_ref[t, k]
            block = vis_ref[b // 8, lax.rem(b, 8)]
            for part in range(2):
                z_ref[pl.ds(t * 128 + part * 8 + k, 8, stride=16), :] = block[
                    part * 16 + h * 8 : part * 16 + h * 8 + 8
                ]
        out_ref[t] = (z_ref[pl.ds(t * 128, 128), :] * 0.0625).astype(BF16)
        return carry

    lax.fori_loop(0, 16, tile, 0)


def rows_phase(got_ref, place_ref, tw_ref, v_ref, y_ref, z_ref):
    def line(i, carry):
        block = got_ref[:, pl.ds(pl.multiple_of(i * 16, 16), 16), :].reshape(256, 128)
        y = nn(place_ref[...], block)
        y = y[:256] + y[256:]
        re, im = y[:128], y[128:]
        cos, sin = tw_ref[0], tw_ref[1]
        at = pl.ds(pl.multiple_of(i * 16, 16), 16)
        y_ref[:, at, 0:128] = (re * cos - im * sin).reshape(8, 16, 128)
        y_ref[:, at, 128:256] = (re * sin + im * cos).reshape(8, 16, 128)
        return carry

    lax.fori_loop(0, 8, line, 0, unroll=2)

    def second(m, carry):
        both = jnp.concatenate([y_ref[2 * m], y_ref[2 * m + 1]], axis=0).astype(BF16)
        out = nt(v_ref[...], both)
        if v_ref.shape[0] == 512:
            out = out[:256] + out[256:]
        for o in range(2):
            for s in range(4):
                z_ref[pl.ds((2 * m + o) * 4 + s, 64, stride=32), :] = out[
                    s * 64 : s * 64 + 64, o * 128 : o * 128 + 128
                ]
        return carry

    lax.fori_loop(0, 4, second, 0)


def main_kernel(
    x_ref, tile_ref, cell_ref, m1_ref, tw1_ref, v1_ref, w_ref, tw2_ref, v2_ref, out_ref,
    z_ref, vis_ref, send_ref, recv_ref, idx_ref, pick_ref, place_ref, blocks_ref, got_ref, y_ref, turned_ref,
    rsend_ref, rrecv_ref, send_sem, recv_sem, pick_sem, bsend_sem, brecv_sem, rsend_sem, rrecv_sem,
):
    me, grp = lax.axis_index("gx"), lax.axis_index("grp")
    greet(me, grp)
    spectra_phase(x_ref, m1_ref, tw1_ref, v1_ref, z_ref)
    pl.semaphore_wait(pltpu.get_barrier_semaphore(), 78)

    def push(step, carry):
        to, _ = by_row(me, step)
        send_ref[to] = z_ref[pl.ds(pl.multiple_of(to * 64, 64), 64), :].astype(BF16)
        gx_copy(send_ref, recv_ref, send_sem, recv_sem, to, me).start()
        return carry

    lax.fori_loop(1, 64, push, 0)
    recv_ref[me] = z_ref[pl.ds(pl.multiple_of(me * 64, 64), 64), :].astype(BF16)

    route_phase(grp, tile_ref, cell_ref, w_ref, idx_ref, place_ref)
    picks = pltpu.make_async_copy(idx_ref, pick_ref, pick_sem)
    picks.start()
    picks.wait()

    def take(step, carry):
        to, source = by_row(me, step)
        gx_copy(send_ref, recv_ref, send_sem, recv_sem, to, source).wait()
        return carry

    row = me // 16
    for dx in range(4):
        lax.fori_loop(max(1, 16 * dx), 16 * dx + 16, take, 0)
        new = lax.rem(row + 4 - dx, 4)

        def against(j, carry, new=new):
            gram_block(recv_ref, vis_ref, new, lax.rem(row + 4 - j, 4))
            return carry

        def under(j, carry, new=new):
            gram_block(recv_ref, vis_ref, lax.rem(row + 4 - j, 4), new)
            return carry

        lax.fori_loop(0, dx + 1, against, 0)
        if dx:
            lax.fori_loop(0, dx, under, 0)

    def block_copy(h, to, slot):
        return grp_copy(
            blocks_ref.at[h], got_ref.at[h], bsend_sem.at[h], brecv_sem.at[h], to, slot
        )

    def push_blocks(h):
        def one(step, carry):
            block_copy(h, lax.rem(grp + step, 16), grp).start()
            return carry

        lax.fori_loop(1, 16, one, 0)
        got_ref[h, grp] = blocks_ref[h, grp]

    def take_blocks(h):
        def one(step, carry):
            block_copy(h, lax.rem(grp + step, 16), lax.rem(grp + 16 - step, 16)).wait()
            return carry

        lax.fori_loop(1, 16, one, 0)

    def row_copy(h, to, slot):
        return gx_copy(
            rsend_ref.at[h], rrecv_ref.at[h], rsend_sem.at[h], rrecv_sem.at[h], to, slot
        )

    def push_rows(h):
        def one(step, carry):
            to, _ = by_distance(me, step)
            rsend_ref[h, to] = z_ref[pl.ds(pl.multiple_of(to * 32, 32), 32), :].astype(BF16)
            row_copy(h, to, me).start()
            return carry

        lax.fori_loop(1, 64, one, 0)
        own = z_ref[pl.ds(pl.multiple_of(me * 32, 32), 32), :].astype(BF16)
        turned_ref[pl.ds(h * 2048 + me, 32, stride=64), :] = own.astype(F32)

    def take_rows(h):
        def one(step, carry):
            to, source = by_distance(me, step)
            row_copy(h, to, source).wait()
            turned_ref[pl.ds(h * 2048 + source, 32, stride=64), :] = rrecv_ref[h, source].astype(F32)
            return carry

        lax.fori_loop(1, 64, one, 0)
        out_ref[h * 2048 : h * 2048 + 2048, :] = turned_ref[h * 2048 : h * 2048 + 2048, :].astype(BF16)

    gather_phase(0, pick_ref, vis_ref, z_ref, blocks_ref.at[0])
    push_blocks(0)
    gather_phase(1, pick_ref, vis_ref, z_ref, blocks_ref.at[1])
    take_blocks(0)
    push_blocks(1)
    rows_phase(got_ref.at[0], place_ref, tw2_ref, v2_ref, y_ref, z_ref)
    push_rows(0)
    take_blocks(1)
    rows_phase(got_ref.at[1], place_ref, tw2_ref, v2_ref, y_ref, z_ref)
    push_rows(1)
    take_rows(0)
    take_rows(1)


def columns_kernel(x_ref, m4_ref, tw_ref, v_ref, image_ref):
    e = pl.program_id(0)
    k2, k1 = e // 2, lax.rem(e, 2)
    turned = []
    for n in range(2):
        for h in range(2):
            x = jnp.concatenate(
                [
                    x_ref[h * 32 + (2 * bit + n) * 8 + k1 * 4 + part * 2 + k2]
                    for part in range(2)
                    for bit in range(2)
                ],
                axis=0,
            )
            t = tn(x, m4_ref[...])
            t = t[:, :256] + t[:, 256:]
            re, im = t[:, :128], t[:, 128:]
            cos, sin = tw_ref[0, n * 2 + h], tw_ref[1, n * 2 + h]
            turned.append((re * cos - im * sin, re * sin + im * cos))
    sides = []
    for side in range(2):
        sides.append(
            jnp.concatenate(
                [
                    turned[nh][part].reshape(8, 2, 8, 128)[:, side].reshape(64, 128)
                    for part in range(2)
                    for nh in range(4)
                ],
                axis=0,
            )
        )
    out = nn(v_ref[...], jnp.concatenate(sides, axis=1).astype(BF16))
    if v_ref.shape[0] == 1024:
        out = out[:512] + out[512:]
    for part in range(2):
        for k in range(32):
            for side in range(2):
                image_ref[part, side * 8 : side * 8 + 8, k * 128 : k * 128 + 128] = out[
                    (part * 32 + k) * 8 : (part * 32 + k) * 8 + 8, side * 128 : side * 128 + 128
                ]


def params(mib, **more):
    return pltpu.CompilerParams(vmem_limit_bytes=mib * 1024 * 1024, **more)


def on_device(voltages, tile_of, cell_of):
    tab = {name: jnp.asarray(value) for name, value in tables().items()}
    vmem = pl.BlockSpec(memory_space=pltpu.VMEM)
    volts = voltages.reshape(16, 2, 128, 128).transpose(0, 2, 1, 3).reshape(16, 256, 128)
    columns = pl.pallas_call(
        main_kernel,
        out_shape=jax.ShapeDtypeStruct((4096, 128), BF16),
        in_specs=[vmem] * 9,
        out_specs=vmem,
        scratch_shapes=[
            pltpu.VMEM((4096, 128), F32),
            pltpu.VMEM((64, 8, 32, 128), F32),
            pltpu.VMEM((64, 64, 128), BF16),
            pltpu.VMEM((64, 64, 128), BF16),
            pltpu.VMEM((16, 128), jnp.int32),
            pltpu.SMEM((16, 128), jnp.int32),
            pltpu.VMEM((512, 256), BF16),
            pltpu.VMEM((2, 16, 128, 128), BF16),
            pltpu.VMEM((2, 16, 128, 128), BF16),
            pltpu.VMEM((8, 128, 256), F32),
            pltpu.VMEM((4096, 128), F32),
            pltpu.VMEM((2, 64, 32, 128), BF16),
            pltpu.VMEM((2, 64, 32, 128), BF16),
            pltpu.SemaphoreType.DMA((64,)),
            pltpu.SemaphoreType.DMA((64,)),
            pltpu.SemaphoreType.DMA,
            pltpu.SemaphoreType.DMA((2, 16)),
            pltpu.SemaphoreType.DMA((2, 16)),
            pltpu.SemaphoreType.DMA((2, 64)),
            pltpu.SemaphoreType.DMA((2, 64)),
        ],
        compiler_params=params(40, collective_id=0, has_side_effects=True),
        name="main",
    )(
        volts, tile_of, cell_of, tab["m1"], tab["tw1"], tab["v1"], tab["w"], tab["tw2"], tab["v2"]
    )
    whole = lambda shape: pl.BlockSpec(shape, lambda e: (0,) * len(shape))
    image = pl.pallas_call(
        columns_kernel,
        grid=(4,),
        out_shape=jax.ShapeDtypeStruct((2, 64, 4096), F32),
        in_specs=[whole(s) for s in ((64, 64, 128), tab["m4"].shape, tab["tw4"].shape, tab["v4"].shape)],
        out_specs=pl.BlockSpec((2, 16, 4096), lambda e: (0, e, 0)),
        compiler_params=params(20),
        name="columns",
    )(columns.reshape(64, 64, 128), tab["m4"], tab["tw4"], tab["v4"])
    return image.reshape(1, 2, 64, 4096)


def solution(mesh):
    in_specs = (P("grp", "gx", None, None, None, None), P(None, "gx"), P(None, "gx"))
    out_specs = P("grp", None, "gx", None)
    return jax.shard_map(
        on_device, mesh=mesh, in_specs=in_specs, out_specs=out_specs, check_vma=False
    )
```

time: 194 us -> 168 us (0.87)
  Pallas kernels: 194 us -> 159 us
  local copies, waits for them, and re-layouts: 0 us -> 8.44 us
    pallas_call x4 -> x2, Pallas kernels: 194 us -> 159 us  [the longest x1 155 us: on_device(): pl.pallas_call(main_kernel, out_shape=jax.ShapeDtypeStruct((4096, 128), B...]
    unnamed x0 -> x24, local copies, waits for them, and re-layouts: none -> 8.44 us
where the time goes in v1:
time: 168 us; the launch traced here: 167 us
  Pallas kernels  159 us (95%)
  local copies, waits for them, and re-layouts  8.44 us (5%)
    pallas_call x1, Pallas kernels, on_device(): pl.pallas_call(main_kernel, out_shape=jax.ShapeDtypeStruct((4096, 128), B...  155 us
    unnamed x24, local copies, waits for them, and re-layouts  8.44 us
    pallas_call x1, Pallas kernels, on_device(): pl.pallas_call(columns_kernel, grid=(4,), out_shape=jax.ShapeDtypeStruct(...  3.88 us

profile of v1, /device:TPU:1, one launch (start us, length us, event | category | flops | bytes accessed | tf_op | source)
XLA Modules:
  0.0 167.2 jit_solution(15071795909373784808)
XLA Ops:
  0.0 0.0 copy-start
  0.0 0.0 copy-start.1
  0.0 1.3 copy-done.1
  1.3 0.0 copy-start.4
  1.3 0.9 copy-done.4
  2.3 0.0 copy-start.5
  2.3 0.9 copy-done.5
  3.2 0.0 copy-start.6
  3.2 0.9 copy-done.6
  4.2 0.0 copy-start.7
  4.2 0.9 copy-done.7
  5.1 0.0 copy-start.8
  5.1 0.9 copy-done.8
  6.0 0.0 copy-start.9
  6.0 0.9 copy-done.9
  6.9 0.0 copy-start.10
  6.9 0.8 copy-done.10
  7.7 0.0 copy-start.11
  7.7 0.8 copy-done.11
  8.4 0.0 copy-start.2
  8.4 0.0 copy-start.3
  8.4 154.9 %main.1 = bf16[4096,128]{1,0:T(8,128)(2,1)S(1)} custom-call(bf16[16,256,128]{2,1,0:T(8,128)(2,1)S(1)} %bitcast.8, s32[16,512]{1,0:T(8,128)S(1)} %copy-done.10, s32[16,512]{1,0:T(8,128)S(1)} %copy-done.11, bf16[512,256]{1,0:T(8,128)(2,1)S(1)} %copy-done.7, f32[2,128,128]{2,1,0:T(8,128)S(1)} %copy-done.9, bf16[512,256]{1,0:T(8,128)(2,1)S(1)} %copy-done.6, ...), custom_call_target="tpu_custom_call" | custom-call | tf_op jit(solution)/shard_map/main/pallas_call | solution.py:405
  163.3 0.0 copy-done
  163.3 0.0 copy-done.2
  163.3 0.0 copy-done.3
  163.3 3.9 %columns.1 = f32[2,64,4096]{2,1,0:T(8,128)} custom-call(bf16[64,64,128]{2,1,0:T(8,128)(2,1)S(1)} %bitcast.7, bf16[256,512]{1,0:T(8,128)(2,1)S(1)} %copy-done.3, f32[2,4,128,128]{3,2,1,0:T(8,128)S(1)} %copy-done.2, bf16[1024,512]{1,0:T(8,128)(2,1)S(1)} %copy-done), custom_call_target="tpu_custom_call" | custom-call | tf_op jit(solution)/shard_map/columns/pallas_call | solution.py:438
Async XLA Ops:
  0.0 163.3 %copy-start = (bf16[1024,512]{1,0:T(8,128)(2,1)S(1)}, bf16[1024,512]{1,0:T(8,128)(2,1)}, u32[]{:S(2)}) copy-start(bf16[1024,512]{1,0:T(8,128)(2,1)} %constant.26.clone.v_ref) | copy-start | bytes 3145732
  0.0 1.3 copy-start.1
  1.3 0.9 copy-start.4
  2.3 0.9 copy-start.5
  3.2 0.9 copy-start.6
  4.2 0.9 copy-start.7
  5.1 0.9 copy-start.8
  6.0 0.9 copy-start.9
  6.9 0.8 copy-start.10
  7.7 0.8 copy-start.11
  8.4 154.9 %copy-start.2 = (f32[2,4,128,128]{3,2,1,0:T(8,128)S(1)}, f32[2,4,128,128]{3,2,1,0:T(8,128)}, u32[]{:S(2)}) copy-start(f32[2,4,128,128]{3,2,1,0:T(8,128)} %constant.25.clone.tw_ref) | copy-start | bytes 1572868
  8.4 154.9 %copy-start.3 = (bf16[256,512]{1,0:T(8,128)(2,1)S(1)}, bf16[256,512]{1,0:T(8,128)(2,1)}, u32[]{:S(2)}) copy-start(bf16[256,512]{1,0:T(8,128)(2,1)} %constant.24.clone.m4_ref) | copy-start | bytes 786436

commit v2 on v1

v2 whole, which is shorter than its diff:
```python
import functools
import math

import jax
import jax.numpy as jnp
import numpy as np
from jax import lax
from jax.experimental import pallas as pl
from jax.experimental.pallas import tpu as pltpu
from jax.sharding import PartitionSpec as P

F32 = jnp.float32
BF16 = jnp.bfloat16
MESH = pl.DeviceIdType.MESH


def split(table):
    high = table.astype(np.float32).astype(jnp.bfloat16)
    low = (table - high.astype(np.float64)).astype(np.float32).astype(jnp.bfloat16)
    return high, low


def turn(left, right, size, sign):
    angle = sign * 2.0 * math.pi / size * (np.outer(left, right) % size)
    return np.cos(angle), np.sin(angle)


@functools.cache
def tables():
    made = {}
    i128 = np.arange(128)
    c, s = turn(i128, i128, 128, -1)
    m1 = np.zeros((2, 128, 128, 2))
    m1[0, :, :, 0], m1[0, :, :, 1] = c, -s
    m1[1, :, :, 0], m1[1, :, :, 1] = s, c
    made["m1"] = np.concatenate(split(m1.reshape(256, 256)))
    made["tw1"] = np.stack(turn(i128, i128, 16384, -1)).astype(np.float32)
    c, s = turn(i128, i128, 128, -1)
    c, s = (t.reshape(64, 2, 128).transpose(1, 0, 2).reshape(128, 128) / 128.0 for t in (c, s))
    made["v1"] = np.concatenate(split(np.block([[c, -s], [s, c]])))
    c, s = turn(np.arange(32), np.arange(32), 32, 1)
    w = np.zeros((2, 4, 32, 2, 4, 32))
    for rb in range(4):
        w[0, rb, :, 0, rb], w[0, rb, :, 1, rb] = c, -s
        w[1, rb, :, 0, rb], w[1, rb, :, 1, rb] = s, c
    made["w"] = np.concatenate(split(w.reshape(256, 256)))
    tw = np.stack(turn(np.arange(32), i128, 4096, 1))
    made["tw2"] = np.tile(tw, (1, 4, 1)).astype(np.float32)
    c, s = turn(i128, i128, 128, 1)
    c, s = (t.reshape(64, 2, 128).transpose(1, 0, 2).reshape(128, 128) / 64.0 for t in (c, s))
    made["v2"] = split(np.block([[c, -s], [s, c]]))[0]
    n1 = (2 * np.arange(64)[None, :] + np.arange(2)[:, None]).reshape(128)
    c, s = turn(n1, i128, 128, 1)
    made["m4"] = np.concatenate(split(np.block([[c, s], [-s, c]])), axis=1)
    n0 = np.arange(32)
    tw = np.stack(turn(n0, i128, 4096, 1)).reshape(2, 8, 4, 1, 128)
    made["tw4"] = np.broadcast_to(tw, (2, 8, 4, 8, 128)).astype(np.float32)
    c, s = turn(n0, n0, 32, 1)
    v4 = np.block([[c, -s], [s, c]]) / 64.0
    made["v4"] = split(np.kron(v4, np.eye(8)))[0]
    return made


def nt(left, right):
    return lax.dot_general(left, right, (((1,), (1,)), ((), ())), preferred_element_type=F32)


def tn(left, right):
    return lax.dot_general(left, right, (((0,), (0,)), ((), ())), preferred_element_type=F32)


def nn(left, right):
    return jnp.dot(left, right, preferred_element_type=F32)


def route_phase(me, tile_ref, cell_ref, w_ref, idx_ref, place_ref):
    tiles = tile_ref[...]
    mine = tile_ref[pl.ds(me, 1), :]
    marks = jnp.concatenate(
        [mine == lax.broadcasted_iota(jnp.int32, (16, 512), 0), tiles == me], axis=0
    ).astype(F32)
    before = lax.broadcasted_iota(jnp.int32, (512, 512), 0) < lax.broadcasted_iota(
        jnp.int32, (512, 512), 1
    )
    rank = nn(marks.astype(BF16), before.astype(F32).astype(BF16))
    rank = jnp.where(marks > 0.5, rank, -1.0).astype(jnp.int32)
    position = lax.broadcasted_iota(jnp.int32, (16, 512), 1)
    columns = [
        jnp.sum(jnp.where(rank[:16] == k, position, 0), axis=1, keepdims=True) for k in range(8)
    ]
    idx_ref[...] = jnp.concatenate(columns + [columns[0]] * 120, axis=1)
    slot = lax.broadcasted_iota(jnp.int32, (8, 512), 0)
    lane = lax.broadcasted_iota(jnp.int32, (8, 256), 1)
    hits = []
    for g in range(16):
        chosen = rank[16 + g : 17 + g] == slot
        cell = jnp.sum(jnp.where(chosen, cell_ref[g : g + 1, :] + 1, 0), axis=1, keepdims=True) - 1
        for part in range(2):
            at = jnp.where(cell < 0, -1, cell + 128 * part)
            hits.append((lane == at).astype(F32))
    onehot = jnp.concatenate(hits, axis=0).astype(BF16)
    place_ref[...] = nt(w_ref[...], onehot).astype(BF16)


def partner(me, dx, d):
    up = (d + 1) // 2
    dz = jnp.where(lax.rem(d, 2) == 1, up, lax.rem(16 - up, 16))
    x, z = me // 16, lax.rem(me, 16)
    to = lax.rem(x + dx, 4) * 16 + lax.rem(z + dz, 16)
    source = lax.rem(x + 4 - dx, 4) * 16 + lax.rem(z + 16 - dz, 16)
    return to, source


def by_row(me, step):
    return partner(me, step // 16, lax.rem(step, 16))


def by_distance(me, step):
    return partner(me, lax.rem(step, 4), step // 4)


def gx_copy(send_ref, recv_ref, send_sem, recv_sem, to, slot):
    return pltpu.make_async_remote_copy(
        src_ref=send_ref.at[to],
        dst_ref=recv_ref.at[slot],
        send_sem=send_sem.at[to],
        recv_sem=recv_sem.at[slot],
        device_id={"gx": to},
        device_id_type=MESH,
    )


def greet(me, grp):
    barrier = pltpu.get_barrier_semaphore()

    def along_gx(step, carry):
        to, _ = by_row(me, step)
        pl.semaphore_signal(barrier, inc=1, device_id={"gx": to}, device_id_type=MESH)
        return carry

    lax.fori_loop(1, 64, along_gx, 0)

    def along_grp(step, carry):
        to = lax.rem(grp + step, 16)
        pl.semaphore_signal(barrier, inc=1, device_id={"grp": to}, device_id_type=MESH)
        return carry

    lax.fori_loop(1, 16, along_grp, 0)


def spectra_phase(four, x_ref, m1_ref, tw_ref, v_ref, z_ref):
    def quad(h, carry):
        four(h)
        cos, sin = tw_ref[0], tw_ref[1]
        for half in range(2):
            first = 4 * h + 2 * half
            y = nn(m1_ref[...], jnp.concatenate([x_ref[first], x_ref[first + 1]], axis=1))
            y = y[:256] + y[256:]
            both = []
            for o in range(2):
                re, im = y[:128, o * 128 : o * 128 + 128], y[128:, o * 128 : o * 128 + 128]
                both.append(jnp.concatenate([re * cos - im * sin, re * sin + im * cos], axis=1))
            both = jnp.concatenate(both, axis=0)
            high = both.astype(BF16)
            low = (both - high.astype(F32)).astype(BF16)
            out = nt(v_ref[...], high)
            out = out[:256] + out[256:] + nt(v_ref[:256], low)
            for o in range(2):
                for s in range(4):
                    z_ref[pl.ds(s * 16 + first + o, 64, stride=64), :] = out[
                        s * 64 : s * 64 + 64, o * 128 : o * 128 + 128
                    ]
        return carry

    lax.fori_loop(0, 4, quad, 0)


def operand(recv_ref, at):
    return jnp.concatenate(
        [recv_ref[pl.ds(at * 16, 16), s * 16 : s * 16 + 16, :].reshape(256, 128) for s in range(4)],
        axis=1,
    )


def gram_block(recv_ref, vis_ref, r, p):
    left, right = operand(recv_ref, r), operand(recv_ref, p)
    crossed = jnp.concatenate([-right[:, 256:], right[:, :256]], axis=1)
    for part, other in enumerate((right, crossed)):
        out = nt(left, other)
        for half in range(2):
            vis_ref[pl.ds(r * 16, 16), 2 * p + half, part * 16 : part * 16 + 16, :] = out[
                :, half * 128 : half * 128 + 128
            ].reshape(16, 16, 128)


def gram_last(recv_ref, vis_ref, new, others):
    right = operand(recv_ref, new)
    crossed = jnp.concatenate([-right[:, 256:], right[:, :256]], axis=1)
    left = jnp.concatenate(
        [recv_ref[:, s * 16 : s * 16 + 16, :].reshape(1024, 128) for s in range(4)], axis=1
    )
    for part, other in enumerate((right, crossed)):
        out = nt(left, other)
        for half in range(2):
            vis_ref[:, 2 * new + half, part * 16 : part * 16 + 16, :] = out[
                :, half * 128 : half * 128 + 128
            ].reshape(64, 16, 128)
    for p in others:
        gram_block(recv_ref, vis_ref, new, p)


def gather_phase(u, idx_ref, vis_ref, z_ref, out_ref):
    def tile(t, carry):
        for k in range(8):
            b = idx_ref[t, k]
            block = vis_ref[b // 8, lax.rem(b, 8)]
            for part in range(2):
                z_ref[pl.ds(t * 64 + part * 8 + k, 4, stride=16), :] = block[
                    part * 16 + u * 4 : part * 16 + u * 4 + 4
                ]
        out_ref[t, u * 64 : u * 64 + 64, :] = (z_ref[pl.ds(t * 64, 64), :] * 0.0625).astype(BF16)
        return carry

    lax.fori_loop(0, 16, tile, 0, unroll=2)


def rows_phase(u, units, local, got_ref, place_ref, tw_ref, v_ref, y_ref, z_ref):
    cos, sin = tw_ref[0], tw_ref[1]
    for i in (0, 2):
        row = (u * 4 + i) * 16
        pair = [got_ref[:, row + o * 16 : row + o * 16 + 16, :].reshape(256, 128) for o in range(2)]
        y = nn(place_ref[...], jnp.concatenate(pair, axis=1))
        y = y[:256] + y[256:]
        for o in range(2):
            re, im = y[:128, o * 128 : o * 128 + 128], y[128:, o * 128 : o * 128 + 128]
            at = slice((i + o) * 32, (i + o) * 32 + 32)
            y_ref[:, at, 0:128] = (re * cos - im * sin).astype(BF16).reshape(4, 32, 128)
            y_ref[:, at, 128:256] = (re * sin + im * cos).astype(BF16).reshape(4, 32, 128)
    for m in (0, 2):
        out = nt(v_ref[...], y_ref[m : m + 2].reshape(256, 256))
        for o in range(2):
            for s in range(4):
                z_ref[pl.ds(local * 16 + (m + o) * 4 + s, 64, stride=16 * units), :] = out[
                    s * 64 : s * 64 + 64, o * 128 : o * 128 + 128
                ]


PARTS = ((0, 1), (1, 1), (2, 2))


def main_kernel(
    x_hbm, tile_hbm, cell_hbm, m1_hbm, tw1_hbm, v1_hbm, w_hbm, tw2_hbm, v2_hbm, out_ref,
    x_ref, tile_ref, cell_ref, m1_ref, tw1_ref, v1_ref, w_ref, tw2_ref, v2_ref,
    z_ref, vis_ref, send_ref, recv_ref, idx_ref, pick_ref, place_ref, blocks_ref, got_ref, y_ref, turned_ref,
    rsend_ref, rrecv_ref, load_sem, four_sem, send_sem, recv_sem, pick_sem, bsend_sem, brecv_sem, rsend_sem, rrecv_sem,
):
    me, grp = lax.axis_index("gx"), lax.axis_index("grp")
    loads = [
        pltpu.make_async_copy(source, target, load_sem.at[n])
        for n, (source, target) in enumerate(
            (
                (m1_hbm, m1_ref), (tw1_hbm, tw1_ref), (v1_hbm, v1_ref), (tile_hbm, tile_ref),
                (cell_hbm, cell_ref), (w_hbm, w_ref), (tw2_hbm, tw2_ref), (v2_hbm, v2_ref),
            )
        )
    ]

    def load_four(h):
        at = pl.ds(h * 4, 4)
        return pltpu.make_async_copy(x_hbm.at[at], x_ref.at[at], four_sem.at[h])

    loads[0].start()
    load_four(0).start()
    loads[1].start()
    loads[2].start()
    for h in range(1, 4):
        load_four(h).start()
    for load in loads[3:]:
        load.start()
    greet(me, grp)
    for load in loads[:3]:
        load.wait()
    spectra_phase(lambda h: load_four(h).wait(), x_ref, m1_ref, tw1_ref, v1_ref, z_ref)
    pl.semaphore_wait(pltpu.get_barrier_semaphore(), 78)

    def push(step, carry):
        to, _ = by_row(me, step)
        send_ref[to] = z_ref[pl.ds(pl.multiple_of(to * 64, 64), 64), :].astype(BF16)
        gx_copy(send_ref, recv_ref, send_sem, recv_sem, to, me).start()
        return carry

    lax.fori_loop(1, 64, push, 0)
    recv_ref[me] = z_ref[pl.ds(pl.multiple_of(me * 64, 64), 64), :].astype(BF16)

    for load in loads[3:]:
        load.wait()
    route_phase(grp, tile_ref, cell_ref, w_ref, idx_ref, place_ref)
    picks = pltpu.make_async_copy(idx_ref, pick_ref, pick_sem)
    picks.start()
    picks.wait()

    def take(step, carry):
        to, source = by_row(me, step)
        gx_copy(send_ref, recv_ref, send_sem, recv_sem, to, source).wait()
        return carry

    row = me // 16
    groups = [lax.rem(row + 4 - dx, 4) for dx in range(4)]
    for dx in range(4):
        lax.fori_loop(max(1, 16 * dx), 16 * dx + 16, take, 0)
        if dx == 3:
            break

        def against(j, carry, dx=dx):
            gram_block(recv_ref, vis_ref, groups[dx], lax.rem(row + 4 - j, 4))
            return carry

        def under(j, carry, dx=dx):
            gram_block(recv_ref, vis_ref, lax.rem(row + 4 - j, 4), groups[dx])
            return carry

        lax.fori_loop(0, dx + 1, against, 0)
        if dx:
            lax.fori_loop(0, dx, under, 0)
    gram_last(recv_ref, vis_ref, groups[3], groups[:3])

    def block_copy(p, to, slot):
        at = pl.ds(PARTS[p][0] * 64, PARTS[p][1] * 64)
        return pltpu.make_async_remote_copy(
            src_ref=blocks_ref.at[to, at],
            dst_ref=got_ref.at[slot, at],
            send_sem=bsend_sem.at[p, to],
            recv_sem=brecv_sem.at[p, slot],
            device_id={"grp": to},
            device_id_type=MESH,
        )

    def push_blocks(p):
        def one(step, carry):
            block_copy(p, lax.rem(grp + step, 16), grp).start()
            return carry

        lax.fori_loop(1, 16, one, 0)
        at = slice(PARTS[p][0] * 64, sum(PARTS[p]) * 64)
        got_ref[grp, at, :] = blocks_ref[grp, at, :]

    def take_blocks(p):
        def one(step, carry):
            block_copy(p, lax.rem(grp + step, 16), lax.rem(grp + 16 - step, 16)).wait()
            return carry

        lax.fori_loop(1, 16, one, 0)

    def row_copy(p, to, slot):
        at = pl.ds(PARTS[p][0] * 16, PARTS[p][1] * 16)
        return pltpu.make_async_remote_copy(
            src_ref=rsend_ref.at[to, at],
            dst_ref=rrecv_ref.at[slot, at],
            send_sem=rsend_sem.at[p, to],
            recv_sem=rrecv_sem.at[p, slot],
            device_id={"gx": to},
            device_id_type=MESH,
        )

    def rows(p):
        first, units = PARTS[p]
        for local in range(units):
            rows_phase(first + local, units, local, got_ref, place_ref, tw2_ref, v2_ref, y_ref, z_ref)

    def push_rows(p):
        first, units = PARTS[p]
        n = units * 16

        def one(step, carry):
            to, _ = by_distance(me, step)
            rsend_ref[to, first * 16 : first * 16 + n, :] = z_ref[
                pl.ds(pl.multiple_of(to * n, n), n), :
            ].astype(BF16)
            row_copy(p, to, me).start()
            return carry

        lax.fori_loop(1, 64, one, 0)
        own = z_ref[pl.ds(pl.multiple_of(me * n, n), n), :].astype(BF16)
        turned_ref[pl.ds(first * 1024 + me, n, stride=64), :] = own.astype(F32)

    def take_rows(p):
        first, units = PARTS[p]
        n = units * 16

        def one(step, carry):
            to, source = by_distance(me, step)
            row_copy(p, to, source).wait()
            turned_ref[pl.ds(first * 1024 + source, n, stride=64), :] = rrecv_ref[
                source, first * 16 : first * 16 + n, :
            ].astype(F32)
            return carry

        lax.fori_loop(1, 64, one, 0)
        at = slice(first * 1024, (first + units) * 1024)
        out_ref[at, :] = turned_ref[at, :].astype(BF16)

    gather_phase(0, pick_ref, vis_ref, z_ref, blocks_ref)
    push_blocks(0)
    for u in range(1, 4):
        gather_phase(u, pick_ref, vis_ref, z_ref, blocks_ref)
    take_blocks(0)
    push_blocks(1)
    push_blocks(2)
    for p in range(3):
        if p:
            take_blocks(p)
        rows(p)
        push_rows(p)
    for p in range(3):
        take_rows(p)


def columns_kernel(x_ref, m4_ref, tw_ref, v_ref, image_ref):
    k2 = pl.program_id(0)
    turned = []
    for n in range(2):
        for u in range(4):
            x = jnp.concatenate(
                [
                    x_ref[u * 16 + (2 * bit + n) * 4 + part * 2 + k2]
                    for part in range(2)
                    for bit in range(2)
                ],
                axis=0,
            )
            t = tn(x, m4_ref[...])
            t = t[:, :256] + t[:, 256:]
            re, im = (t[:, o * 128 : o * 128 + 128].reshape(4, 4, 8, 128) for o in range(2))
            cos, sin = (tw_ref[o, n * 4 + u].reshape(4, 1, 8, 128) for o in range(2))
            turned.append((re * cos - im * sin, re * sin + im * cos))
    for pair in (0, 2):
        sides = [
            jnp.concatenate(
                [turned[nu][part][:, side].reshape(32, 128) for part in range(2) for nu in range(8)],
                axis=0,
            )
            for side in (pair, pair + 1)
        ]
        out = nn(v_ref[...], jnp.concatenate(sides, axis=1).astype(BF16))
        for part in range(2):
            for k in range(32):
                for o in range(2):
                    at = (pair + o) * 8
                    image_ref[part, at : at + 8, k * 128 : k * 128 + 128] = out[
                        (part * 32 + k) * 8 : (part * 32 + k) * 8 + 8, o * 128 : o * 128 + 128
                    ]


def params(mib, **more):
    return pltpu.CompilerParams(vmem_limit_bytes=mib * 1024 * 1024, **more)


def on_device(voltages, tile_of, cell_of):
    tab = {name: jnp.asarray(value) for name, value in tables().items()}
    vmem = pl.BlockSpec(memory_space=pltpu.VMEM)
    volts = voltages.reshape(16, 2, 128, 128).transpose(0, 2, 1, 3).reshape(16, 256, 128)
    columns = pl.pallas_call(
        main_kernel,
        out_shape=jax.ShapeDtypeStruct((4096, 128), BF16),
        in_specs=[pl.BlockSpec(memory_space=pltpu.HBM)] * 9,
        out_specs=vmem,
        scratch_shapes=[
            pltpu.VMEM((16, 256, 128), BF16),
            pltpu.VMEM((16, 512), jnp.int32),
            pltpu.VMEM((16, 512), jnp.int32),
            *(pltpu.VMEM(tab[name].shape, tab[name].dtype) for name in ("m1", "tw1", "v1", "w", "tw2", "v2")),
            pltpu.VMEM((4096, 128), F32),
            pltpu.VMEM((64, 8, 32, 128), F32),
            pltpu.VMEM((64, 64, 128), BF16),
            pltpu.VMEM((64, 64, 128), BF16),
            pltpu.VMEM((16, 128), jnp.int32),
            pltpu.SMEM((16, 128), jnp.int32),
            pltpu.VMEM((512, 256), BF16),
            pltpu.VMEM((16, 256, 128), BF16),
            pltpu.VMEM((16, 256, 128), BF16),
            pltpu.VMEM((4, 128, 256), BF16),
            pltpu.VMEM((4096, 128), F32),
            pltpu.VMEM((64, 64, 128), BF16),
            pltpu.VMEM((64, 64, 128), BF16),
            pltpu.SemaphoreType.DMA((8,)),
            pltpu.SemaphoreType.DMA((4,)),
            pltpu.SemaphoreType.DMA((64,)),
            pltpu.SemaphoreType.DMA((64,)),
            pltpu.SemaphoreType.DMA,
            pltpu.SemaphoreType.DMA((3, 16)),
            pltpu.SemaphoreType.DMA((3, 16)),
            pltpu.SemaphoreType.DMA((3, 64)),
            pltpu.SemaphoreType.DMA((3, 64)),
        ],
        compiler_params=params(40, collective_id=0, has_side_effects=True),
        name="main",
    )(
        *(
            pltpu.with_memory_space_constraint(array, pltpu.HBM)
            for array in (
                volts, tile_of, cell_of, tab["m1"], tab["tw1"], tab["v1"], tab["w"], tab["tw2"], tab["v2"]
            )
        )
    )
    whole = lambda shape: pl.BlockSpec(shape, lambda e: (0,) * len(shape))
    image = pl.pallas_call(
        columns_kernel,
        grid=(2,),
        out_shape=jax.ShapeDtypeStruct((2, 64, 4096), F32),
        in_specs=[whole(s) for s in ((64, 64, 128), tab["m4"].shape, tab["tw4"].shape, tab["v4"].shape)],
        out_specs=pl.BlockSpec((2, 32, 4096), lambda e: (0, e, 0)),
        compiler_params=params(20),
        name="columns",
    )(columns.reshape(64, 64, 128), tab["m4"], tab["tw4"], tab["v4"])
    return image.reshape(1, 2, 64, 4096)


def solution(mesh):
    in_specs = (P("grp", "gx", None, None, None, None), P(None, "gx"), P(None, "gx"))
    out_specs = P("grp", None, "gx", None)
    return jax.shard_map(
        on_device, mesh=mesh, in_specs=in_specs, out_specs=out_specs, check_vma=False
    )
```

time: 168 us -> 150 us (0.89)
  Pallas kernels: 159 us -> 149 us
  local copies, waits for them, and re-layouts: 8.44 us -> 0.01 us
    unnamed x24 -> x6, local copies, waits for them, and re-layouts: 8.44 us -> 0.01 us
    pallas_call x1, Pallas kernels: 155 us -> 147 us  [on_device(): pl.pallas_call(main_kernel, out_shape=jax.ShapeDtypeStruct((4096, 128), B...]
where the time goes in v2:
time: 150 us; the launch traced here: 149 us
  Pallas kernels  149 us (99%)
    pallas_call x1, Pallas kernels, on_device(): pl.pallas_call(main_kernel, out_shape=jax.ShapeDtypeStruct((4096, 128), B...  147 us

profile of v2, /device:TPU:1, one launch (start us, length us, event | category | flops | bytes accessed | tf_op | source)
XLA Modules:
  0.0 149.5 jit_solution(8084198428917430816)
XLA Ops:
  0.0 0.0 copy-start
  0.0 0.0 copy-start.1
  0.0 0.0 copy-start.2
  0.0 146.7 %main.1 = bf16[4096,128]{1,0:T(8,128)(2,1)S(1)} custom-call(bf16[16,256,128]{2,1,0:T(8,128)(2,1)} %bitcast.8, s32[16,512]{1,0:T(8,128)} %tile_hbm.1, s32[16,512]{1,0:T(8,128)} %cell_hbm.1, bf16[512,256]{1,0:T(8,128)(2,1)} %constant.18.clone.m1_hbm, f32[2,128,128]{2,1,0:T(8,128)} %constant.19.clone.tw1_hbm, bf16[512,256]{1,0:T(8,128)(2,1)} %constant.20.clone.v1_hbm, ...), custom_call_target="tpu_custom_call" | custom-call | tf_op jit(solution)/shard_map/main/pallas_call | solution.py:462
  146.7 0.0 copy-done
  146.7 0.0 copy-done.1
  146.7 0.0 copy-done.2
  146.7 2.8 %columns.1 = f32[2,64,4096]{2,1,0:T(8,128)} custom-call(bf16[64,64,128]{2,1,0:T(8,128)(2,1)S(1)} %bitcast.7, bf16[256,512]{1,0:T(8,128)(2,1)S(1)} %copy-done.2, f32[2,8,4,8,128]{4,3,2,1,0:T(8,128)S(1)} %copy-done.1, bf16[512,512]{1,0:T(8,128)(2,1)S(1)} %copy-done), custom_call_target="tpu_custom_call" | custom-call | tf_op jit(solution)/shard_map/columns/pallas_call | solution.py:506
Async XLA Ops:
  0.0 146.7 %copy-start = (bf16[512,512]{1,0:T(8,128)(2,1)S(1)}, bf16[512,512]{1,0:T(8,128)(2,1)}, u32[]{:S(2)}) copy-start(bf16[512,512]{1,0:T(8,128)(2,1)} %constant.26.clone.v_ref) | copy-start | bytes 1572868
  0.0 146.7 %copy-start.1 = (f32[2,8,4,8,128]{4,3,2,1,0:T(8,128)S(1)}, f32[2,8,4,8,128]{4,3,2,1,0:T(8,128)}, u32[]{:S(2)}) copy-start(f32[2,8,4,8,128]{4,3,2,1,0:T(8,128)} %constant.25.clone.tw_ref) | copy-start | bytes 786436
  0.0 146.7 %copy-start.2 = (bf16[256,512]{1,0:T(8,128)(2,1)S(1)}, bf16[256,512]{1,0:T(8,128)(2,1)}, u32[]{:S(2)}) copy-start(bf16[256,512]{1,0:T(8,128)(2,1)} %constant.24.clone.m4_ref) | copy-start | bytes 786436

commit v3 on v2

--- a/solution.py
+++ b/solution.py
@@ -119,6 +119,20 @@
     return partner(me, lax.rem(step, 4), step // 4)
 
 
+def by_start(me, step):
+    dx = lax.rem(step, 4)
+    d = step // 4
+    z = lax.rem(me, 16)
+    i = d // 2
+    wrapped = jnp.maximum(z - 7, 0)
+    up = jnp.where(i < wrapped, i, z + 1 + i - wrapped)
+    low = jnp.maximum(z - 7, 0)
+    j = i - 1
+    down = jnp.where(j < z - low, low + j, z + 9 + j - (z - low))
+    zt = jnp.where(lax.rem(d, 2) == 1, up, jnp.where(d == 0, z, down))
+    return lax.rem(me // 16 + dx, 4) * 16 + zt
+
+
 def gx_copy(send_ref, recv_ref, send_sem, recv_sem, to, slot):
     return pltpu.make_async_remote_copy(
         src_ref=send_ref.at[to],
@@ -245,7 +259,7 @@
                 ]
 
 
-PARTS = ((0, 1), (1, 1), (2, 2))
+PARTS = ((0, 2), (2, 2))
 
 
 def main_kernel(
@@ -372,7 +386,7 @@
         n = units * 16
 
         def one(step, carry):
-            to, _ = by_distance(me, step)
+            to = by_start(me, step)
             rsend_ref[to, first * 16 : first * 16 + n, :] = z_ref[
                 pl.ds(pl.multiple_of(to * n, n), n), :
             ].astype(BF16)
@@ -399,19 +413,19 @@
         at = slice(first * 1024, (first + units) * 1024)
         out_ref[at, :] = turned_ref[at, :].astype(BF16)
 
-    gather_phase(0, pick_ref, vis_ref, z_ref, blocks_ref)
+    for u in range(2):
+        gather_phase(u, pick_ref, vis_ref, z_ref, blocks_ref)
     push_blocks(0)
-    for u in range(1, 4):
+    for u in range(2, 4):
         gather_phase(u, pick_ref, vis_ref, z_ref, blocks_ref)
     take_blocks(0)
     push_blocks(1)
-    push_blocks(2)
-    for p in range(3):
+    for p in range(2):
         if p:
             take_blocks(p)
         rows(p)
         push_rows(p)
-    for p in range(3):
+    for p in range(2):
         take_rows(p)
 
 
@@ -487,10 +501,10 @@
             pltpu.SemaphoreType.DMA((64,)),
             pltpu.SemaphoreType.DMA((64,)),
             pltpu.SemaphoreType.DMA,
-            pltpu.SemaphoreType.DMA((3, 16)),
-            pltpu.SemaphoreType.DMA((3, 16)),
-            pltpu.SemaphoreType.DMA((3, 64)),
-            pltpu.SemaphoreType.DMA((3, 64)),
+            pltpu.SemaphoreType.DMA((2, 16)),
+            pltpu.SemaphoreType.DMA((2, 16)),
+            pltpu.SemaphoreType.DMA((2, 64)),
+            pltpu.SemaphoreType.DMA((2, 64)),
         ],
         compiler_params=params(40, collective_id=0, has_side_effects=True),
         name="main",

time: 150 us -> 147 us (0.980); the launches traced: 149 us -> 144 us
  Pallas kernels: 149 us -> 144 us
    pallas_call x1, Pallas kernels: 147 us -> 142 us  [on_device(): pl.pallas_call(main_kernel, out_shape=jax.ShapeDtypeStruct((4096, 128), B...]
where the time goes in v3:
time: 147 us; the launch traced here: 144 us
  Pallas kernels  144 us (98%)
    pallas_call x1, Pallas kernels, on_device(): pl.pallas_call(main_kernel, out_shape=jax.ShapeDtypeStruct((4096, 128), B...  142 us

profile of v3, /device:TPU:1, one launch (start us, length us, event | category | flops | bytes accessed | tf_op | source)
XLA Modules:
  0.0 144.4 jit_solution(16060512162263397298)
XLA Ops:
  0.0 0.0 copy-start
  0.0 0.0 copy-start.1
  0.0 0.0 copy-start.2
  0.0 141.6 %main.1 = bf16[4096,128]{1,0:T(8,128)(2,1)S(1)} custom-call(bf16[16,256,128]{2,1,0:T(8,128)(2,1)} %bitcast.8, s32[16,512]{1,0:T(8,128)} %tile_hbm.1, s32[16,512]{1,0:T(8,128)} %cell_hbm.1, bf16[512,256]{1,0:T(8,128)(2,1)} %constant.18.clone.m1_hbm, f32[2,128,128]{2,1,0:T(8,128)} %constant.19.clone.tw1_hbm, bf16[512,256]{1,0:T(8,128)(2,1)} %constant.20.clone.v1_hbm, ...), custom_call_target="tpu_custom_call" | custom-call | tf_op jit(solution)/shard_map/main/pallas_call | solution.py:476
  141.6 0.0 copy-done
  141.6 0.0 copy-done.1
  141.6 0.0 copy-done.2
  141.6 2.8 %columns.1 = f32[2,64,4096]{2,1,0:T(8,128)} custom-call(bf16[64,64,128]{2,1,0:T(8,128)(2,1)S(1)} %bitcast.7, bf16[256,512]{1,0:T(8,128)(2,1)S(1)} %copy-done.2, f32[2,8,4,8,128]{4,3,2,1,0:T(8,128)S(1)} %copy-done.1, bf16[512,512]{1,0:T(8,128)(2,1)S(1)} %copy-done), custom_call_target="tpu_custom_call" | custom-call | tf_op jit(solution)/shard_map/columns/pallas_call | solution.py:520
Async XLA Ops:
  0.0 141.6 %copy-start = (bf16[512,512]{1,0:T(8,128)(2,1)S(1)}, bf16[512,512]{1,0:T(8,128)(2,1)}, u32[]{:S(2)}) copy-start(bf16[512,512]{1,0:T(8,128)(2,1)} %constant.26.clone.v_ref) | copy-start | bytes 1572868
  0.0 141.6 %copy-start.1 = (f32[2,8,4,8,128]{4,3,2,1,0:T(8,128)S(1)}, f32[2,8,4,8,128]{4,3,2,1,0:T(8,128)}, u32[]{:S(2)}) copy-start(f32[2,8,4,8,128]{4,3,2,1,0:T(8,128)} %constant.25.clone.tw_ref) | copy-start | bytes 786436
  0.0 141.6 %copy-start.2 = (bf16[256,512]{1,0:T(8,128)(2,1)S(1)}, bf16[256,512]{1,0:T(8,128)(2,1)}, u32[]{:S(2)}) copy-start(bf16[256,512]{1,0:T(8,128)(2,1)} %constant.24.clone.m4_ref) | copy-start | bytes 786436
